TPU v7x, 32 devices: a whole 2x2x4 slice. The times are simulated.
32 devices in a mesh: tmpl: 16 (over z, x, core), tm: 2 (over y).
Axes of the slice: x: 2, y: 2, z: 4, core: 2. Of those that a mesh axis runs over, the one named last changes fastest.
Arguments:
- records: bfloat16 [1536, 1024], P('tmpl', 'tm'), may hold values from -6 to 6
- templates: bfloat16 [2, 512, 48, 200], P(None, 'tmpl'), may hold values from -0.0625 to 0.0625
- channels: int32 [2, 512, 48], P(None, 'tmpl'), may hold values from 0 to 1535
- moveouts: int32 [2, 512, 48], P(None, 'tmpl'), may hold values from 0 to 55
Outputs:
- detections: float32 [2, 512, 1024], P(None, 'tmpl', 'tm')
All inputs are finite; a program needn't handle non-finite values.
Results may differ from a plain program's by a relative error of at most 0.0043.
Values may be sent and summed in bfloat16 or wider, within the bound.
A program may use at most 64 MiB of HBM per device.

v0:
```python
import math

import jax
import jax.numpy as jnp
from jax import lax
from jax.sharding import PartitionSpec as P

L = 200
LAGS = 56


def from_behind(block, axis, distance):
    devices = range(lax.axis_size(axis))
    route = [(i - distance, i) for i in devices if i - distance in devices]
    return lax.ppermute(block, axis, route)


def tables(count, freqs, width):
    sample = jnp.arange(count, dtype=jnp.int32)[:, None]
    freq = jnp.arange(freqs, dtype=jnp.int32)[None, :]
    angle = 2.0 * math.pi / width * (sample * freq % width).astype(jnp.float32)
    return jnp.concatenate([jnp.cos(angle), jnp.sin(angle)], axis=1)


def detect(waves, chans, lags, spectra, forward, inverse, weight, freq, width, freqs):
    count = waves.shape[0]
    hspec = jnp.dot(
        waves.reshape(-1, waves.shape[2]),
        forward[: waves.shape[2]],
        preferred_element_type=jnp.float32,
    )
    h_cos, h_sin = (hspec[:, :freqs], hspec[:, freqs:])
    angle = (
        2.0
        * math.pi
        / width
        * (lags.reshape(-1)[:, None] * freq[None, :] % width).astype(jnp.float32)
    )
    c_theta, s_theta = (jnp.cos(angle), jnp.sin(angle))
    picked = spectra[chans.reshape(-1)].astype(jnp.float32)
    x_cos, x_sin = (picked[:, :freqs], picked[:, freqs:])
    prod_a = h_cos * x_cos + h_sin * x_sin
    prod_b = h_sin * x_cos - h_cos * x_sin
    real_part = (prod_a * c_theta - prod_b * s_theta).reshape(count, -1, freqs).sum(axis=1)
    imag_part = (prod_a * s_theta + prod_b * c_theta).reshape(count, -1, freqs).sum(axis=1)
    joint = jnp.concatenate([real_part * weight, -imag_part * weight], axis=1)
    return lax.dot_general(
        joint, inverse, (((1,), (1,)), ((), ())), precision=lax.Precision.HIGHEST
    )


def per_device(records, templates, channels, moveouts):
    time_dev = records.shape[1]
    extra = L + LAGS - 2
    width = time_dev + extra
    freqs = width // 2 + 1
    forward = tables(width, freqs, width).astype(jnp.bfloat16)
    inverse = tables(time_dev, freqs, width)
    freq = jnp.arange(freqs, dtype=jnp.int32)
    weight = jnp.where((freq == 0) | (freq == freqs - 1), 1.0, 2.0).astype(jnp.float32) / width
    rim = from_behind(records[:, :extra], "tm", -1)
    window = jnp.concatenate([records, rim], axis=1)
    spectra = jnp.dot(
        lax.all_gather(window, "tmpl", axis=0, tiled=True),
        forward,
        preferred_element_type=jnp.float32,
    ).astype(jnp.bfloat16)
    results = []
    for batch in range(templates.shape[0]):
        results.append(
            detect(
                templates[batch],
                channels[batch],
                moveouts[batch],
                spectra,
                forward,
                inverse,
                weight,
                freq,
                width,
                freqs,
            )
        )
    return jnp.stack(results)


def solution(mesh):
    placed = (
        P("tmpl", "tm"),
        P(None, "tmpl", None, None),
        P(None, "tmpl", None),
        P(None, "tmpl", None),
    )
    return jax.shard_map(
        per_device, mesh=mesh, in_specs=placed, out_specs=P(None, "tmpl", "tm"), check_vma=False
    )
```

profile of v0, /device:TPU:0, one launch (start us, length us, event | category | flops | bytes accessed | tf_op | source)
XLA Modules:
  0.0 160.1 jit_solution(14229189575895089181)
XLA Ops:
  6.5 0.0 all-gather.2.cloned.1.call-start
  6.5 0.8 slice.52
  7.3 1.3 collective-permute-start
  8.6 5.0 %collective-permute-done = bf16[96,254]{1,0:T(8,128)(2,1)S(1)} collective-permute-done((bf16[96,254]{1,0:T(8,128)(2,1)S(1)}, bf16[96,254]{1,0:T(8,128)(2,1)S(1)}, u32[]{:S(2)}, u32[]{:S(2)}) %collective-permute-start) | collective-permute-done | bytes 48800 | tf_op jit(solution)/shard_map/ppermute | solution.py:15
  13.6 1.6 pad_maximum_fusion.8
  15.2 0.0 all-gather.2.cloned.1.call-update
  15.2 0.9 fusion.46
  16.1 0.1 reshape_squeeze.15
  16.2 0.7 fusion.47
  16.9 0.1 mul.198
  17.0 0.1 reshape_squeeze.13
  17.1 0.1 mul.177
  17.3 5.0 %sine_convert_fusion = (bf16[766,384]{1,0:T(8,128)(2,1)S(1)}, bf16[766,384]{1,0:T(8,128)(2,1)S(1)}) fusion(), kind=kLoop, calls=%fused_computation.41 | loop fusion | flops 3235584 | bytes 1176576 | tf_op jit(solution)/shard_map/convert.1
  22.3 0.0 copy-start.3
  22.3 0.0 copy-start.4
  22.3 0.8 copy-done.3
  23.1 0.3 copy-done.4
  23.3 4.2 %fusion.30 = (f32[512,384]{1,0:T(8,128)S(1)}, f32[512,384]{1,0:T(8,128)}) fusion(), kind=kLoop, calls=%fused_computation.54 | loop fusion | flops 1769472 | bytes 1572864 | tf_op jit(solution)/shard_map/sin | solution.py:22
  27.6 0.0 copy-done.5
  27.6 0.1 fusion.45
  27.7 3.0 %convolution_bitcast_fusion = f32[1536,768]{0,1:T(8,128)} fusion(bf16[200,768]{1,0:T(8,128)(2,1)S(1)} %pad_maximum_fusion.7, bf16[1536,200]{1,0:T(8,128)(2,1)S(1)} %bitcast.24), kind=kOutput, calls=%fused_computation.2 | convolution fusion | flops 471859200 | bytes 5640192 | tf_op jit(solution)/shard_map/dot_general | solution.py:27
  30.7 3.0 %convolution_bitcast_fusion.1 = f32[1536,768]{0,1:T(8,128)} fusion(bf16[200,768]{1,0:T(8,128)(2,1)S(1)} %pad_maximum_fusion.7, bf16[1536,200]{1,0:T(8,128)(2,1)S(1)} %bitcast.23), kind=kOutput, calls=%fused_computation.3 | convolution fusion | flops 471859200 | bytes 5640192 | tf_op jit(solution)/shard_map/dot_general | solution.py:27
  33.7 25.5 %all-gather.2.cloned.1.call-done = bf16[1536,766]{1,0:T(8,128)(2,1)} async-done(((bf16[96,766]{1,0:T(8,128)(2,1)}), bf16[1536,766]{1,0:T(8,128)(2,1)}) %all-gather.2.cloned.1.call-update) | async-done | bytes 2353168 | tf_op jit(solution)/shard_map/all_gather | solution.py:64
  59.1 4.0 %convolution_convert_fusion = bf16[1536,768]{1,0:T(8,128)(2,1)S(1)} fusion(bf16[1536,766]{1,0:T(8,128)(2,1)} %all-gather.2.cloned.1.call-done, bf16[766,384]{1,0:T(8,128)(2,1)} %copy-done.3, bf16[766,384]{1,0:T(8,128)(2,1)} %copy-done.4), kind=kOutput, calls=%fused_computation.6 | convolution fusion | flops 1810753536 | bytes 5889024 | tf_op jit(solution)/shard_map/dot_general | solution.py:63
  63.1 5.7 %gather_fusion.1 = bf16[1536,768]{1,0:T(8,128)(2,1)} fusion(bf16[1536,768]{1,0:T(8,128)(2,1)S(1)} %convolution_convert_fusion, s32[2048]{0:T(1024)S(1)} %pad_clamp_fusion), kind=kCustom, calls=%fused_computation.1 | custom fusion | bytes 4724736 | tf_op jit(solution)/shard_map/gather | solution.py:40
  68.8 4.3 %copy.10 = bf16[1536,768]{0,1:T(8,128)(2,1)} copy(bf16[1536,768]{1,0:T(8,128)(2,1)} %gather_fusion.1) | data formatting | bytes 4718592 | tf_op jit(solution)/shard_map/gather | solution.py:40
  73.0 2.3 %convert_element_type.31 = f32[1536,768]{0,1:T(8,128)S(1)} convert(bf16[1536,768]{0,1:T(8,128)(2,1)} %copy.10) | non-fusion elementwise | flops 1179648 | bytes 7077888 | tf_op jit(solution)/shard_map/convert_element_type | solution.py:40
  75.3 13.5 %multiply_subtract_fusion = (f32[1536,384]{0,1:T(8,128)}, f32[1536,384]{0,1:T(8,128)S(1)}, f32[1536,384]{0,1:T(8,128)S(1)}) fusion(s32[1536]{0:T(1024)S(1)} %mul.198, f32[1536,768]{0,1:T(8,128)S(1)} %convert_element_type.31, f32[1536,768]{0,1:T(8,128)} %convolution_bitcast_fusion), kind=kLoop, calls=%fused_computation.12 | loop fusion | flops 10616832 | bytes 16521216 | tf_op jit(solution)/shard_map/sub | solution.py:44
  88.9 10.8 %multiply_add_fusion = f32[1536,384]{0,1:T(8,128)} fusion(f32[1536,384]{0,1:T(8,128)S(1)} %get-tuple-element.10, f32[1536,384]{0,1:T(8,128)S(1)} %get-tuple-element.9, s32[1536]{0:T(1024)S(1)} %mul.198), kind=kLoop, calls=%fused_computation.11 | loop fusion | flops 7077888 | bytes 7084032 | tf_op jit(solution)/shard_map/add | solution.py:45
  99.6 3.1 %copy.12 = f32[1536,384]{1,0:T(8,128)} copy(f32[1536,384]{0,1:T(8,128)} %multiply_add_fusion) | data formatting | bytes 4718592 | tf_op jit(solution)/shard_map/add | solution.py:45
  102.8 5.7 %gather_fusion = bf16[1536,768]{1,0:T(8,128)(2,1)} fusion(bf16[1536,768]{1,0:T(8,128)(2,1)S(1)} %convolution_convert_fusion, s32[2048]{0:T(1024)S(1)} %pad_clamp_fusion.1), kind=kCustom, calls=%fused_computation | custom fusion | bytes 4724736 | tf_op jit(solution)/shard_map/gather | solution.py:40
  108.4 2.8 %copy.7 = bf16[1536,768]{0,1:T(8,128)(2,1)S(1)} copy(bf16[1536,768]{1,0:T(8,128)(2,1)} %gather_fusion) | data formatting | bytes 4718592 | tf_op jit(solution)/shard_map/gather | solution.py:40
  111.3 0.6 convert_element_type.28
  111.9 13.5 %multiply_subtract_fusion.2 = (f32[1536,384]{0,1:T(8,128)}, f32[1536,384]{0,1:T(8,128)S(1)}, f32[1536,384]{0,1:T(8,128)S(1)}) fusion(s32[1536]{0:T(1024)S(1)} %mul.177, f32[1536,768]{0,1:T(8,128)S(1)} %convert_element_type.28, f32[1536,768]{0,1:T(8,128)} %convolution_bitcast_fusion.1), kind=kLoop, calls=%fused_computation.21 | loop fusion | flops 10616832 | bytes 16521216 | tf_op jit(solution)/shard_map/sub | solution.py:44
  125.5 9.9 %multiply_add_fusion.2 = f32[1536,384]{0,1:T(8,128)S(1)} fusion(f32[1536,384]{0,1:T(8,128)S(1)} %get-tuple-element.7, f32[1536,384]{0,1:T(8,128)S(1)} %get-tuple-element.6, s32[1536]{0:T(1024)S(1)} %mul.177), kind=kLoop, calls=%fused_computation.20 | loop fusion | flops 7077888 | bytes 7084032 | tf_op jit(solution)/shard_map/add | solution.py:45
  135.3 2.0 %copy.9 = f32[1536,384]{1,0:T(8,128)} copy(f32[1536,384]{0,1:T(8,128)S(1)} %multiply_add_fusion.2) | data formatting | bytes 4718592 | tf_op jit(solution)/shard_map/add | solution.py:45
  137.3 2.0 %reduce_sum.39 = f32[32,384]{1,0:T(8,128)S(1)} reduce(f32[32,48,384]{2,1,0:T(8,128)} %bitcast.19, f32[]{:T(128)} %constant.26.clone.1), dimensions={1}, to_apply=%region_3.4 | reduce | flops 577536 | bytes 2408452 | tf_op jit(solution)/shard_map/reduce_sum | solution.py:45
  139.3 1.9 %reduce_sum.37 = f32[32,384]{1,0:T(8,128)S(1)} reduce(f32[32,48,384]{2,1,0:T(8,128)} %bitcast.20, f32[]{:T(128)} %constant.26.clone.1), dimensions={1}, to_apply=%region_1.2 | reduce | flops 577536 | bytes 2408452 | tf_op jit(solution)/shard_map/reduce_sum | solution.py:45
  141.2 0.0 copy-done
  141.2 2.0 %copy.11 = f32[1536,384]{1,0:T(8,128)} copy(f32[1536,384]{0,1:T(8,128)S(1)} %copy-done) | data formatting | bytes 4718592 | tf_op jit(solution)/shard_map/sub | solution.py:44
  143.2 2.0 %reduce_sum.38 = f32[32,384]{1,0:T(8,128)S(1)} reduce(f32[32,48,384]{2,1,0:T(8,128)} %bitcast.22, f32[]{:T(128)} %constant.26.clone.1), dimensions={1}, to_apply=%region_2.3 | reduce | flops 577536 | bytes 2408452 | tf_op jit(solution)/shard_map/reduce_sum | solution.py:44
  145.2 0.4 copy-done.1
  145.5 2.0 %copy.8 = f32[1536,384]{1,0:T(8,128)} copy(f32[1536,384]{0,1:T(8,128)S(1)} %copy-done.1) | data formatting | bytes 4718592 | tf_op jit(solution)/shard_map/sub | solution.py:44
  147.5 1.9 %reduce_sum.36 = f32[32,384]{1,0:T(8,128)S(1)} reduce(f32[32,48,384]{2,1,0:T(8,128)} %bitcast.21, f32[]{:T(128)} %constant.26.clone.1), dimensions={1}, to_apply=%region_0.1 | reduce | flops 577536 | bytes 2408452 | tf_op jit(solution)/shard_map/reduce_sum | solution.py:44
  149.5 0.0 copy-done.2
  149.5 1.5 fusion.24
  151.0 1.5 fusion.25
  152.6 0.7 pad_maximum_fusion.9
  (11 shorter events, 0.1 us)
Async XLA Ops:
  6.5 52.6 %all-gather.2.cloned.1.call-start = ((), (), s32[]{:S(2)}) async-start(), calls=%async_computation | async-start | bytes 2506752 | tf_op jit(solution)/shard_map/all_gather | solution.py:64
  7.3 6.3 %collective-permute-start = (bf16[96,254]{1,0:T(8,128)(2,1)S(1)}, bf16[96,254]{1,0:T(8,128)(2,1)S(1)}, u32[]{:S(2)}, u32[]{:S(2)}) collective-permute-start(bf16[96,254]{1,0:T(8,128)(2,1)S(1)} %slice.52), channel_id=1, source_target_pairs={{1,0},{3,2},{5,4},{7,6},{9,8},{11,10},{13,12},{15,14},{17,16},{19,... | collective-permute-start | bytes 146312 | tf_op jit(solution)/shard_map/ppermute | solution.py:15
  15.2 12.4 %copy-start.5 = (bf16[2,32,48,200]{3,2,1,0:T(8,128)(2,1)S(1)}, bf16[2,32,48,200]{3,2,1,0:T(8,128)(2,1)}, u32[]{:S(2)}) copy-start(bf16[2,32,48,200]{3,2,1,0:T(8,128)(2,1)} %param.5) | copy-start | bytes 3686404
  22.3 0.8 copy-start.3
  22.3 1.1 copy-start.4
  137.3 3.9 %copy-start = (f32[1536,384]{0,1:T(8,128)S(1)}, f32[1536,384]{0,1:T(8,128)}, u32[]{:S(2)}) copy-start(f32[1536,384]{0,1:T(8,128)} %get-tuple-element.8) | copy-start | bytes 7077892
  143.2 2.4 %copy-start.1 = (f32[1536,384]{0,1:T(8,128)S(1)}, f32[1536,384]{0,1:T(8,128)}, u32[]{:S(2)}) copy-start(f32[1536,384]{0,1:T(8,128)} %get-tuple-element.5) | copy-start | bytes 7077892
  147.5 2.0 %copy-start.2 = (f32[512,384]{1,0:T(8,128)S(1)}, f32[512,384]{1,0:T(8,128)}, u32[]{:S(2)}) copy-start(f32[512,384]{1,0:T(8,128)} %get-tuple-element.24) | copy-start | bytes 2359300
Sparse Core Ops, SparseCore 0:
  15.4 43.7 all-gather.1
where the time goes:
time: 161 us; the launch traced here: 160 us
  other arithmetic  70 us (43%)
  local copies, waits for them, and re-layouts  31.7 us (20%)
  waiting for transfers between devices  30.5 us (19%)
  between operations  13.6 us (8%)
  matrix products  13 us (8%)
    sub x2, other arithmetic, detect(): prod_a * c_theta - prod_b * s_theta  27.1 us
    all_gather x1, waiting for transfers between devices, per_device(): lax.all_gather(window, 'tmpl', axis=0, tiled=True)  25.5 us
    add x2, other arithmetic, detect(): prod_a * s_theta + prod_b * c_theta  20.6 us
    gather x4, local copies, waits for them, and re-layouts, detect(): picked = spectra[chans.reshape(-1)].astype(jnp.float32)  18.4 us
    dot_general x2, matrix products, detect(): jnp.dot(waves.reshape(-1, waves.shape[2]), forward[:waves.shape[2]], pref...  5.99 us
    add x2, local copies, waits for them, and re-layouts, detect(): prod_a * s_theta + prod_b * c_theta  5.11 us
    ppermute x1, waiting for transfers between devices, from_behind(): return lax.ppermute(block, axis, route)  5.01 us
    another operation x1, other arithmetic  5 us
  transfers between devices with their start and end apart: 2, of which 2 were waited for; matrix products, arithmetic and copies ran while one was open for 11% of the time, Pallas kernels for 0%

commit v1 on v0

v1 whole, which is shorter than its diff:
```python
import functools
import math

import jax
import jax.numpy as jnp
import ml_dtypes
import numpy as np
from jax import lax
from jax.experimental import pallas as pl
from jax.experimental.pallas import tpu as pltpu
from jax.sharding import PartitionSpec as P

L = 200
LAGS = 56
SPAN = 256
LANES = 128
SLOTS = 8


def from_behind(block, axis, distance):
    devices = range(lax.axis_size(axis))
    route = [(i - distance, i) for i in devices if i - distance in devices]
    return lax.ppermute(block, axis, route)


def tables(count, freqs, width):
    turn = np.arange(count, dtype=np.int64)[:, None] * np.arange(freqs, dtype=np.int64)[None, :]
    angle = 2.0 * math.pi / width * (turn % width).astype(np.float64)
    return np.concatenate([np.cos(angle), np.sin(angle)], axis=1)


def spread(dst, first, rows, values, slots):
    for piece, slot in enumerate(slots):
        dst[pl.ds(first * SLOTS + slot, rows, stride=SLOTS), :] = values[
            :, piece * LANES : (piece + 1) * LANES
        ]


def waves_spectra(waves_ref, lags_ref, basis_ref, h_ref, rows):
    def step(i, carry):
        first = pl.multiple_of(i * rows, rows)
        wave = waves_ref[pl.ds(first, rows), :].astype(jnp.float32)
        lag = jnp.broadcast_to(lags_ref[pl.ds(first, rows), :], (rows, SPAN))
        bit = 1
        while bit < LAGS:
            wave = jnp.where((lag & bit) != 0, pltpu.roll(wave, bit, 1), wave)
            bit *= 2
        spec = jnp.dot(
            wave.astype(jnp.bfloat16), basis_ref[:SPAN, :], preferred_element_type=jnp.float32
        )
        spread(h_ref, first, rows, spec, (0, 1, 2, 4, 5, 6))
        return carry

    lax.fori_loop(0, waves_ref.shape[0] // rows, step, 0)


def record_spectra(window_ref, basis_ref, x_ref, y_ref, rows):
    def step(i, carry):
        first = pl.multiple_of(i * rows, rows)
        spec = jnp.dot(
            window_ref[pl.ds(first, rows), :], basis_ref[...], preferred_element_type=jnp.float32
        )
        spec = spec.astype(jnp.bfloat16).astype(jnp.float32)
        spread(x_ref, first, rows, spec, (0, 1, 2, 4, 5, 6))
        spread(y_ref, first, rows, spec, (4, 5, 6, 0, 1, 2))
        return carry

    lax.fori_loop(0, window_ref.shape[0] // rows, step, 0)


def correlate(chans_ref, h_ref, x_ref, y_ref, p_ref, q_ref, count, parts):
    def step(t, carry):
        same = [None] * 4
        cross = [None] * 4
        for k in range(parts):
            row = t * parts + k
            chan = pl.multiple_of(chans_ref[row] * SLOTS, SLOTS)
            h = h_ref[pl.ds(pl.multiple_of(row * SLOTS, SLOTS), SLOTS), :]
            a = h * x_ref[pl.ds(chan, SLOTS), :]
            b = h * y_ref[pl.ds(chan, SLOTS), :]
            lane = k % 4
            same[lane] = a if same[lane] is None else same[lane] + a
            cross[lane] = b if cross[lane] is None else cross[lane] + b
        at = pl.ds(pl.multiple_of(t * SLOTS, SLOTS), SLOTS)
        p_ref[at, :] = (same[0] + same[1]) + (same[2] + same[3])
        q_ref[at, :] = (cross[0] + cross[1]) + (cross[2] + cross[3])
        return carry

    lax.fori_loop(0, count, step, 0)


def back(p_ref, q_ref, inverse_ref, out_ref, count):
    real, imag = [], []
    for j in range(3):
        low, high = pl.ds(j, count, stride=SLOTS), pl.ds(j + 4, count, stride=SLOTS)
        real.append(p_ref[low, :] + p_ref[high, :])
        imag.append(q_ref[low, :] - q_ref[high, :])
    joint = jnp.concatenate(real + imag, axis=1)
    out_ref[...] = lax.dot_general(
        joint,
        inverse_ref[...],
        (((1,), (0,)), ((), ())),
        precision=lax.Precision.HIGHEST,
        preferred_element_type=jnp.float32,
    )


def kernel(
    count, parts, chans_ref, window_ref, waves_ref, lags_ref, basis_ref, inverse_ref, out_ref,
    h_ref, x_ref, y_ref, p_ref, q_ref,
):
    waves_spectra(waves_ref, lags_ref, basis_ref, h_ref, 256)
    record_spectra(window_ref, basis_ref, x_ref, y_ref, 256)
    correlate(chans_ref, h_ref, x_ref, y_ref, p_ref, q_ref, count, parts)
    back(p_ref, q_ref, inverse_ref, out_ref, count)


def per_device(records, templates, channels, moveouts):
    time_dev = records.shape[1]
    extra = L + LAGS - 2
    width = time_dev + extra
    freqs = width // 2 + 1
    wide = time_dev + SPAN
    batches, count, parts = channels.shape
    total = batches * count
    rows = total * parts
    forward = np.zeros((wide, 2 * freqs), np.float32)
    forward[:width] = tables(width, freqs, width)
    basis = jnp.asarray(forward.astype(ml_dtypes.bfloat16))
    freq = np.arange(freqs)
    weight = np.where((freq == 0) | (freq == freqs - 1), 1.0, 2.0) / width
    inverse = jnp.asarray(
        (tables(time_dev, freqs, width) * np.concatenate([weight, weight])).T.astype(np.float32)
    )
    rim = from_behind(records[:, :SPAN], "tm", -1)
    window = lax.all_gather(jnp.concatenate([records, rim], axis=1), "tmpl", axis=0, tiled=True)
    waves = jnp.pad(templates.reshape(rows, L), ((0, 0), (0, SPAN - L)))
    vmem = pl.BlockSpec(memory_space=pltpu.VMEM)
    out = pl.pallas_call(
        functools.partial(kernel, total, parts),
        out_shape=jax.ShapeDtypeStruct((total, time_dev), jnp.float32),
        in_specs=[pl.BlockSpec(memory_space=pltpu.SMEM)] + [vmem] * 5,
        out_specs=vmem,
        scratch_shapes=[
            pltpu.VMEM((rows * SLOTS, LANES), jnp.float32),
            pltpu.VMEM((window.shape[0] * SLOTS, LANES), jnp.float32),
            pltpu.VMEM((window.shape[0] * SLOTS, LANES), jnp.float32),
            pltpu.VMEM((total * SLOTS, LANES), jnp.float32),
            pltpu.VMEM((total * SLOTS, LANES), jnp.float32),
        ],
        compiler_params=pltpu.CompilerParams(vmem_limit_bytes=52 * 2**20),
    )(channels.reshape(rows), window, waves, moveouts.reshape(rows, 1), basis, inverse)
    return out.reshape(batches, count, time_dev)


def solution(mesh):
    placed = (
        P("tmpl", "tm"),
        P(None, "tmpl", None, None),
        P(None, "tmpl", None),
        P(None, "tmpl", None),
    )
    return jax.shard_map(
        per_device, mesh=mesh, in_specs=placed, out_specs=P(None, "tmpl", "tm"), check_vma=False
    )
```

time: 161 us -> 90.3 us (0.56)
  other arithmetic: 70 us -> 1.57 us
  local copies, waits for them, and re-layouts: 31.7 us -> 5.86 us
  Pallas kernels: 0 us -> 23.9 us
  waiting for transfers between devices: 30.5 us -> 44 us
  matrix products: 13 us -> 0 us
    sub x2 -> x0, other arithmetic: 27.1 us -> none  [detect(): prod_a * c_theta - prod_b * s_theta]
    pallas_call x0 -> x1, Pallas kernels: none -> 23.9 us  [per_device(): pl.pallas_call(functools.partial(kernel, total, parts), out_shape=jax.Sha...]
    add x2 -> x0, other arithmetic: 20.6 us -> none  [detect(): prod_a * s_theta + prod_b * c_theta]
    gather x4 -> x0, local copies, waits for them, and re-layouts: 18.4 us -> none  [detect(): picked = spectra[chans.reshape(-1)].astype(jnp.float32)]
    all_gather x1, waiting for transfers between devices: 25.5 us -> 39 us  [per_device(): lax.all_gather(jnp.concatenate([records, rim], axis=1), 'tmpl', axis=0, t...]
    dot_general x5 -> x0, matrix products: 13 us -> none  [the longest x2 5.99 us: detect(): jnp.dot(waves.reshape(-1, waves.shape[2]), forward[:waves.shape[2]], pref...]
    reduce_sum x4 -> x0, other arithmetic: 7.81 us -> none  [the longest x2 3.94 us: detect(): (prod_a * c_theta - prod_b * s_theta).reshape(count, -1, freqs).sum(axis=1)]
    another operation x2 -> x0, other arithmetic: 5.67 us -> none
  transfers between devices with their start and end apart: 2 -> 2, of which waited for: 2 -> 2; matrix products, arithmetic and copies ran while one was open for 11% -> 5% of each run, Pallas kernels for 0% -> 0%
where the time goes in v1:
time: 90.3 us; the launch traced here: 90 us
  waiting for transfers between devices  44 us (49%)
  Pallas kernels  23.9 us (26%)
  between operations  13.4 us (15%)
  local copies, waits for them, and re-layouts  5.86 us (6%)
  other arithmetic  1.57 us (2%)
  starting transfers between devices  1.28 us (1%)
    all_gather x1, waiting for transfers between devices, per_device(): lax.all_gather(jnp.concatenate([records, rim], axis=1), 'tmpl', axis=0, t...  39 us
    pallas_call x1, Pallas kernels, per_device(): pl.pallas_call(functools.partial(kernel, total, parts), out_shape=jax.Sha...  23.9 us
    ppermute x1, waiting for transfers between devices, from_behind(): return lax.ppermute(block, axis, route)  5.01 us
    reshape x1, local copies, waits for them, and re-layouts, per_device(): moveouts.reshape(rows, 1)  2.71 us
  transfers between devices with their start and end apart: 2, of which 2 were waited for; matrix products, arithmetic and copies ran while one was open for 5% of the time, Pallas kernels for 0%

profile of v1, /device:TPU:0, one launch (start us, length us, event | category | flops | bytes accessed | tf_op | source)
XLA Modules:
  0.0 90.0 jit_solution(16785564860924376470)
XLA Ops:
  6.5 0.0 copy-start.1
  6.5 0.0 all-gather.2.cloned.1.call-start
  6.5 0.9 %slice.3 = bf16[96,256]{1,0:T(8,128)(2,1)S(1)} slice(bf16[96,512]{1,0:T(8,128)(2,1)} %param.6), slice={[0:96], [0:256]} | slice | bytes 98304 | tf_op jit(solution)/shard_map/slice | solution.py:135
  7.5 1.3 %collective-permute-start = (bf16[96,256]{1,0:T(8,128)(2,1)S(1)}, bf16[96,256]{1,0:T(8,128)(2,1)S(1)}, u32[]{:S(2)}, u32[]{:S(2)}) collective-permute-start(bf16[96,256]{1,0:T(8,128)(2,1)S(1)} %slice.3), channel_id=1, source_target_pairs={{1,0},{3,2},{5,4},{7,6},{9,8},{11,10},{13,12},{15,14},{17,16},{19,... | collective-permute-start | bytes 147464 | tf_op jit(solution)/shard_map/ppermute | solution.py:23
  8.7 5.0 %collective-permute-done = bf16[96,256]{1,0:T(8,128)(2,1)S(1)} collective-permute-done((bf16[96,256]{1,0:T(8,128)(2,1)S(1)}, bf16[96,256]{1,0:T(8,128)(2,1)S(1)}, u32[]{:S(2)}, u32[]{:S(2)}) %collective-permute-start) | collective-permute-done | bytes 49184 | tf_op jit(solution)/shard_map/ppermute | solution.py:23
  13.8 1.6 %pad_maximum_fusion = bf16[96,768]{1,0:T(8,128)(2,1)} fusion(bf16[96,256]{1,0:T(8,128)(2,1)S(1)} %collective-permute-done, bf16[96,512]{1,0:T(8,128)(2,1)} %param.6), kind=kLoop, calls=%fused_computation | loop fusion | flops 294912 | bytes 294912 | tf_op jit(solution)/shard_map/concatenate | solution.py:136
  15.3 0.0 all-gather.2.cloned.1.call-update
  15.4 0.8 reshape.12.chans_ref
  16.2 2.7 %reshape.16.lags_ref = s32[3072,1]{1,0:T(8,128)} reshape(s32[2,32,48]{2,1,0:T(8,128)} %param.9) | data formatting | bytes 24576 | tf_op jit(solution)/shard_map/reshape | solution.py:152
  18.9 0.0 copy-done.1
  18.9 0.0 copy-start
  18.9 1.4 %pad.4.waves_ref = bf16[3072,256]{1,0:T(8,128)(2,1)} pad(bf16[3072,200]{1,0:T(8,128)(2,1)S(1)} %bitcast.2, bf16[]{:T(256)} %constant.6.clone.1), padding=0_0x0_56 | pad | bytes 2801666 | tf_op jit(solution)/shard_map/jit(_pad)/pad | solution.py:137
  20.3 39.0 %all-gather.2.cloned.1.call-done.window_ref = bf16[1536,768]{1,0:T(8,128)(2,1)} async-done(((bf16[96,768]{1,0:T(8,128)(2,1)}), bf16[1536,768]{1,0:T(8,128)(2,1)}) %all-gather.2.cloned.1.call-update) | async-done | bytes 2359312 | tf_op jit(solution)/shard_map/all_gather | solution.py:136
  59.2 0.0 copy-done
  59.2 23.9 %shard_map.64 = f32[64,512]{1,0:T(8,128)} custom-call(s32[3072]{0:T(1024)S(1)} %reshape.12.chans_ref, bf16[1536,768]{1,0:T(8,128)(2,1)} %all-gather.2.cloned.1.call-done.window_ref, bf16[3072,256]{1,0:T(8,128)(2,1)} %pad.4.waves_ref, s32[3072,1]{1,0:T(8,128)} %reshape.16.lags_ref, bf16[768,768]{1,0:T(8,128)(2,1)S(1)} %copy-done, ...), custom_call_target="tpu_custom_call" | custom-call | tf_op jit(solution)/shard_map/pallas_call | solution.py:139
Async XLA Ops:
  6.5 12.4 %copy-start.1 = (bf16[2,32,48,200]{3,2,1,0:T(8,128)(2,1)S(1)}, bf16[2,32,48,200]{3,2,1,0:T(8,128)(2,1)}, u32[]{:S(2)}) copy-start(bf16[2,32,48,200]{3,2,1,0:T(8,128)(2,1)} %param.7) | copy-start | bytes 3686404
  6.5 52.7 %all-gather.2.cloned.1.call-start = ((), (), s32[]{:S(2)}) async-start(), calls=%async_computation | async-start | bytes 2506752 | tf_op jit(solution)/shard_map/all_gather | solution.py:136
  7.5 6.3 %collective-permute-start = (bf16[96,256]{1,0:T(8,128)(2,1)S(1)}, bf16[96,256]{1,0:T(8,128)(2,1)S(1)}, u32[]{:S(2)}, u32[]{:S(2)}) collective-permute-start(bf16[96,256]{1,0:T(8,128)(2,1)S(1)} %slice.3), channel_id=1, source_target_pairs={{1,0},{3,2},{5,4},{7,6},{9,8},{11,10},{13,12},{15,14},{17,16},{19,... | collective-permute-start | bytes 147464 | tf_op jit(solution)/shard_map/ppermute | solution.py:23
  18.9 40.3 %copy-start = (bf16[768,768]{1,0:T(8,128)(2,1)S(1)}, bf16[768,768]{1,0:T(8,128)(2,1)}, u32[]{:S(2)}) copy-start(bf16[768,768]{1,0:T(8,128)(2,1)} %constant.7.clone.basis_ref) | copy-start | bytes 3538948
Sparse Core Ops, SparseCore 0:
  15.5 43.7 all-gather.1

commit v2 on v1

--- a/solution.py
+++ b/solution.py
@@ -14,13 +14,133 @@
 LAGS = 56
 SPAN = 256
 LANES = 128
+OUTER = 4
 SLOTS = 8
 
 
-def from_behind(block, axis, distance):
-    devices = range(lax.axis_size(axis))
-    route = [(i - distance, i) for i in devices if i - distance in devices]
-    return lax.ppermute(block, axis, route)
+class Gather:
+    def __init__(self, win, send, recv, devices, windows, rows, time_dev):
+        self.win, self.send, self.recv = win, send, recv
+        self.rows, self.time_dev = rows, time_dev
+        self.outer, self.inner = OUTER, devices // (2 * OUTER)
+        me = lax.axis_index("tmpl")
+        self.me, self.core = me, me % 2
+        self.o, self.m = me // (2 * self.inner), me // 2 % self.inner
+        self.tm, self.windows = lax.axis_index("tm"), windows
+        self.turns = (0, 1, 3, 2)
+        self.sent = []
+
+    def index(self, k, j, core):
+        o = (self.o - k + self.outer) % self.outer
+        m = (self.m - j + self.inner) % self.inner
+        return (o * self.inner + m) * 2 + core
+
+    def block(self, k, j, core, first, columns):
+        at = pl.multiple_of(self.index(k, j, core) * self.rows, self.rows)
+        return self.win.at[pl.ds(at, self.rows), pl.ds(first, columns)]
+
+    def copy(self, kind, k, j, ref, target):
+        at = (kind * self.outer + k) * self.inner + j
+        return pltpu.make_async_remote_copy(
+            src_ref=ref,
+            dst_ref=ref,
+            send_sem=self.send.at[at],
+            recv_sem=self.recv.at[at],
+            device_id=target,
+            device_id_type=pl.DeviceIdType.MESH,
+        )
+
+    def main(self, k, j):
+        if j == 0:
+            return self.copy(
+                0, k, j, self.block(0, 0, self.core, 0, self.time_dev),
+                (self.index(-k, 0, self.core), self.tm),
+            )
+        return self.copy(
+            0, k, j, self.block(k, 0, self.core, 0, self.time_dev),
+            (self.index(0, -j, self.core), self.tm),
+        )
+
+    def rim(self, k, j):
+        ref = self.block(k, j, self.core, 0, SPAN)
+        at = (self.outer + k) * self.inner + j
+        return pltpu.make_async_remote_copy(
+            src_ref=ref,
+            dst_ref=self.block(k, j, self.core, self.time_dev, SPAN),
+            send_sem=self.send.at[at],
+            recv_sem=self.recv.at[at],
+            device_id=(self.me, (self.tm + self.windows - 1) % self.windows),
+            device_id_type=pl.DeviceIdType.MESH,
+        )
+
+    def across(self, k, j):
+        return self.copy(
+            2, k, j, self.block(k, j, self.core, 0, self.time_dev + SPAN),
+            (self.index(0, 0, 1 - self.core), self.tm),
+        )
+
+    def go(self, copy):
+        copy.start()
+        self.sent.append(copy)
+
+    def greet(self):
+        barrier = pltpu.get_barrier_semaphore()
+        peers = [(self.index(-k, 0, self.core), self.tm) for k in range(1, self.outer)]
+        peers += [(self.index(0, -j, self.core), self.tm) for j in range(1, self.inner)]
+        peers += [(self.index(0, 0, 1 - self.core), self.tm)]
+        peers += [(self.me, (self.tm + 1) % self.windows)]
+        for peer in peers:
+            pl.semaphore_signal(
+                barrier, inc=1, device_id=peer, device_id_type=pl.DeviceIdType.MESH
+            )
+        pl.semaphore_wait(barrier, len(peers))
+
+    def own(self, records_ref):
+        at = pl.multiple_of(self.me * self.rows, self.rows)
+        self.win[pl.ds(at, self.rows), pl.ds(0, self.time_dev)] = records_ref[...]
+
+    def run(self, beside=lambda: None):
+        for k in self.turns[1:]:
+            self.go(self.main(k, 0))
+        for k in self.turns:
+            if k:
+                beside()
+                self.main(k, 0).wait_recv()
+            for j in range(1, self.inner):
+                self.go(self.main(k, j))
+            self.go(self.rim(k, 0))
+        for j in range(1, self.inner):
+            for k in self.turns:
+                beside()
+                self.main(k, j).wait_recv()
+                self.go(self.rim(k, j))
+        for j in range(self.inner):
+            for k in self.turns:
+                beside()
+                self.rim(k, j).wait_recv()
+                self.go(self.across(k, j))
+
+    def finish(self):
+        for j in range(self.inner):
+            for k in self.turns:
+                self.across(k, j).wait_recv()
+        for copy in self.sent:
+            copy.wait_send()
+
+        @pl.when(self.tm == self.windows - 1)
+        def _():
+            rim = self.win.shape[0], SPAN
+            self.win[:, pl.ds(self.time_dev, SPAN)] = jnp.zeros(rim, self.win.dtype)
+
+
+def gather_kernel(devices, windows, records_ref, out_ref, win, send, recv):
+    rows, time_dev = records_ref.shape
+    moves = Gather(win, send, recv, devices, windows, rows, time_dev)
+    moves.own(records_ref)
+    moves.greet()
+    moves.run()
+    moves.finish()
+    out_ref[...] = win[...]
 
 
 def tables(count, freqs, width):
@@ -132,8 +252,22 @@
     inverse = jnp.asarray(
         (tables(time_dev, freqs, width) * np.concatenate([weight, weight])).T.astype(np.float32)
     )
-    rim = from_behind(records[:, :SPAN], "tm", -1)
-    window = lax.all_gather(jnp.concatenate([records, rim], axis=1), "tmpl", axis=0, tiled=True)
+    devices, windows = lax.axis_size("tmpl"), lax.axis_size("tm")
+    copies = 3 * devices // 2
+    window = pl.pallas_call(
+        functools.partial(gather_kernel, devices, windows),
+        out_shape=jax.ShapeDtypeStruct((devices * records.shape[0], wide), records.dtype),
+        in_specs=[pl.BlockSpec(memory_space=pltpu.VMEM)],
+        out_specs=pl.BlockSpec(memory_space=pltpu.VMEM),
+        scratch_shapes=[
+            pltpu.VMEM((devices * records.shape[0], wide), records.dtype),
+            pltpu.SemaphoreType.DMA((copies,)),
+            pltpu.SemaphoreType.DMA((copies,)),
+        ],
+        compiler_params=pltpu.CompilerParams(
+            collective_id=0, has_side_effects=True, vmem_limit_bytes=24 * 2**20
+        ),
+    )(records)
     waves = jnp.pad(templates.reshape(rows, L), ((0, 0), (0, SPAN - L)))
     vmem = pl.BlockSpec(memory_space=pltpu.VMEM)
     out = pl.pallas_call(

time: 90.3 us -> 54.9 us (0.61)
  waiting for transfers between devices: 44 us -> 0 us
  Pallas kernels: 23.9 us -> 47.7 us
  between operations: 13.4 us -> 0.02 us
  other arithmetic: 1.57 us -> 0 us
  starting transfers between devices: 1.28 us -> 0 us
  local copies, waits for them, and re-layouts: 5.86 us -> 7.03 us
    all_gather x1 -> x0, waiting for transfers between devices: 39 us -> none  [per_device(): lax.all_gather(jnp.concatenate([records, rim], axis=1), 'tmpl', axis=0, t...]
    pallas_call x0 -> x1, Pallas kernels: none -> 23.8 us  [per_device(): pl.pallas_call(functools.partial(gather_kernel, devices, windows), out_sh...]
    ppermute x1 -> x0, waiting for transfers between devices: 5.01 us -> none  [from_behind(): return lax.ppermute(block, axis, route)]
    concatenate x1 -> x0, other arithmetic: 1.57 us -> none  [per_device(): jnp.concatenate([records, rim], axis=1)]
    pad x1, local copies, waits for them, and re-layouts: 1.39 us -> 2.82 us  [per_device(): waves = jnp.pad(templates.reshape(rows, L), ((0, 0), (0, SPAN - L)))]
    unnamed x4 -> x8, local copies, waits for them, and re-layouts: 0.01 us -> 1.43 us
    ppermute x1 -> x0, starting transfers between devices: 1.28 us -> none  [from_behind(): return lax.ppermute(block, axis, route)]
    slice x1 -> x0, local copies, waits for them, and re-layouts: 0.92 us -> none  [per_device(): rim = from_behind(records[:, :SPAN], 'tm', -1)]
  transfers between devices with their start and end apart: 2 -> 0, of which waited for: 2 -> 0; matrix products, arithmetic and copies ran while one was open for 5% -> 0% of each run, Pallas kernels for 0% -> 0%
where the time goes in v2:
time: 54.9 us; the launch traced here: 54.7 us
  Pallas kernels  47.7 us (87%)
  local copies, waits for them, and re-layouts  7.03 us (13%)
    pallas_call x1, Pallas kernels, per_device(): pl.pallas_call(functools.partial(kernel, total, parts), out_shape=jax.Sha...  23.9 us
    pallas_call x1, Pallas kernels, per_device(): pl.pallas_call(functools.partial(gather_kernel, devices, windows), out_sh...  23.8 us
    pad x1, local copies, waits for them, and re-layouts, per_device(): waves = jnp.pad(templates.reshape(rows, L), ((0, 0), (0, SPAN - L)))  2.82 us
    reshape x1, local copies, waits for them, and re-layouts, per_device(): moveouts.reshape(rows, 1)  1.96 us
    unnamed x8, local copies, waits for them, and re-layouts  1.43 us

profile of v2, /device:TPU:0, one launch (start us, length us, event | category | flops | bytes accessed | tf_op | source)
XLA Modules:
  0.0 54.7 jit_solution(16704340508852060517)
XLA Ops:
  0.0 0.8 %reshape.12.chans_ref = s32[3072]{0:T(1024)S(1)} reshape(s32[2,32,48]{2,1,0:T(8,128)} %param.8) | data formatting | bytes 24576 | tf_op jit(solution)/shard_map/reshape | solution.py:286
  0.8 0.0 copy-start.3
  0.8 2.8 %pad.4.waves_ref = bf16[3072,256]{1,0:T(8,128)(2,1)} pad(bf16[3072,200]{1,0:T(8,128)(2,1)} %bitcast.2, bf16[]{:T(256)} %constant.6.clone.1), padding=0_0x0_56 | pad | bytes 2801666 | tf_op jit(solution)/shard_map/jit(_pad)/pad | solution.py:271
  3.7 0.0 copy-done.3
  3.7 0.0 copy-start.2
  3.7 2.0 %reshape.16.lags_ref = s32[3072,1]{1,0:T(8,128)} reshape(s32[2,32,48]{2,1,0:T(8,128)S(1)} %copy-done.3) | data formatting | bytes 24576 | tf_op jit(solution)/shard_map/reshape | solution.py:286
  5.6 0.0 copy-done.2
  5.6 0.0 copy-start.1
  5.6 23.8 %shard_map.64.window_ref = bf16[1536,768]{1,0:T(8,128)(2,1)S(1)} custom-call(bf16[96,512]{1,0:T(8,128)(2,1)S(1)} %copy-done.2), custom_call_target="tpu_custom_call" | custom-call | tf_op jit(solution)/shard_map/pallas_call | solution.py:257
  29.4 0.0 copy-start
  29.4 1.4 %copy-done = bf16[1536,768]{1,0:T(8,128)(2,1)} copy-done((bf16[1536,768]{1,0:T(8,128)(2,1)}, bf16[1536,768]{1,0:T(8,128)(2,1)S(1)}, u32[]{:S(2)}) %copy-start) | copy-done | bytes 2359320
  30.8 0.0 copy-done.1
  30.8 23.9 %shard_map.65 = f32[64,512]{1,0:T(8,128)} custom-call(s32[3072]{0:T(1024)S(1)} %reshape.12.chans_ref, bf16[1536,768]{1,0:T(8,128)(2,1)} %copy-done, bf16[3072,256]{1,0:T(8,128)(2,1)} %pad.4.waves_ref, s32[3072,1]{1,0:T(8,128)} %reshape.16.lags_ref, bf16[768,768]{1,0:T(8,128)(2,1)S(1)} %copy-done.1, f32[768,512]{1,0:T(8,128)} %constant.8.clone.inverse_ref), custom_call_target="tpu_custom_call" | custom-call | tf_op jit(solution)/shard_map/pallas_call | solution.py:273
Async XLA Ops:
  0.8 2.8 %copy-start.3 = (s32[2,32,48]{2,1,0:T(8,128)S(1)}, s32[2,32,48]{2,1,0:T(8,128)}, u32[]{:S(2)}) copy-start(s32[2,32,48]{2,1,0:T(8,128)} %param.9) | copy-start | bytes 36868
  3.7 2.0 %copy-start.2 = (bf16[96,512]{1,0:T(8,128)(2,1)S(1)}, bf16[96,512]{1,0:T(8,128)(2,1)}, u32[]{:S(2)}) copy-start(bf16[96,512]{1,0:T(8,128)(2,1)} %records_ref.1) | copy-start | bytes 294916
  5.6 25.2 %copy-start.1 = (bf16[768,768]{1,0:T(8,128)(2,1)S(1)}, bf16[768,768]{1,0:T(8,128)(2,1)}, u32[]{:S(2)}) copy-start(bf16[768,768]{1,0:T(8,128)(2,1)} %constant.7.clone.basis_ref) | copy-start | bytes 3538948
  29.4 1.4 %copy-start = (bf16[1536,768]{1,0:T(8,128)(2,1)}, bf16[1536,768]{1,0:T(8,128)(2,1)S(1)}, u32[]{:S(2)}) copy-start(bf16[1536,768]{1,0:T(8,128)(2,1)S(1)} %shard_map.64.window_ref) | copy-start | bytes 7077892

commit v3 on v2

--- a/solution.py
+++ b/solution.py
@@ -15,6 +15,7 @@
 SPAN = 256
 LANES = 128
 OUTER = 4
+CHUNK = 4
 SLOTS = 8
 
 
@@ -133,16 +134,6 @@
             self.win[:, pl.ds(self.time_dev, SPAN)] = jnp.zeros(rim, self.win.dtype)
 
 
-def gather_kernel(devices, windows, records_ref, out_ref, win, send, recv):
-    rows, time_dev = records_ref.shape
-    moves = Gather(win, send, recv, devices, windows, rows, time_dev)
-    moves.own(records_ref)
-    moves.greet()
-    moves.run()
-    moves.finish()
-    out_ref[...] = win[...]
-
-
 def tables(count, freqs, width):
     turn = np.arange(count, dtype=np.int64)[:, None] * np.arange(freqs, dtype=np.int64)[None, :]
     angle = 2.0 * math.pi / width * (turn % width).astype(np.float64)
@@ -156,22 +147,26 @@
         ]
 
 
-def waves_spectra(waves_ref, lags_ref, basis_ref, h_ref, rows):
-    def step(i, carry):
-        first = pl.multiple_of(i * rows, rows)
-        wave = waves_ref[pl.ds(first, rows), :].astype(jnp.float32)
-        lag = jnp.broadcast_to(lags_ref[pl.ds(first, rows), :], (rows, SPAN))
-        bit = 1
-        while bit < LAGS:
-            wave = jnp.where((lag & bit) != 0, pltpu.roll(wave, bit, 1), wave)
-            bit *= 2
-        spec = jnp.dot(
-            wave.astype(jnp.bfloat16), basis_ref[:SPAN, :], preferred_element_type=jnp.float32
-        )
-        spread(h_ref, first, rows, spec, (0, 1, 2, 4, 5, 6))
-        return carry
-
-    lax.fori_loop(0, waves_ref.shape[0] // rows, step, 0)
+def waves_spectra(waves_ref, lags_ref, basis_ref, h_ref, parts, chunk):
+    rows = CHUNK * parts
+    first = chunk * rows
+    wave = waves_ref[pl.ds(first, rows), :].astype(jnp.float32)
+    wave = jnp.concatenate([wave, jnp.zeros((rows, SPAN - L), jnp.float32)], axis=1)
+    square = (parts, parts)
+    eye = lax.broadcasted_iota(jnp.int32, square, 0) == lax.broadcasted_iota(jnp.int32, square, 1)
+    lags = []
+    for t in range(chunk * CHUNK, (chunk + 1) * CHUNK):
+        across = jnp.broadcast_to(lags_ref[pl.ds(t, 1), :].astype(jnp.float32), square)
+        lags.append(jnp.sum(jnp.where(eye, across, 0.0), axis=1, keepdims=True))
+    lag = jnp.broadcast_to(jnp.concatenate(lags, axis=0).astype(jnp.int32), (rows, SPAN))
+    bit = 1
+    while bit < LAGS:
+        wave = jnp.where((lag & bit) != 0, pltpu.roll(wave, bit, 1), wave)
+        bit *= 2
+    spec = jnp.dot(
+        wave.astype(jnp.bfloat16), basis_ref[:SPAN, :], preferred_element_type=jnp.float32
+    )
+    spread(h_ref, first, rows, spec, (0, 1, 2, 4, 5, 6))
 
 
 def record_spectra(window_ref, basis_ref, x_ref, y_ref, rows):
@@ -194,7 +189,7 @@
         cross = [None] * 4
         for k in range(parts):
             row = t * parts + k
-            chan = pl.multiple_of(chans_ref[row] * SLOTS, SLOTS)
+            chan = chans_ref[t, k] * SLOTS
             h = h_ref[pl.ds(pl.multiple_of(row * SLOTS, SLOTS), SLOTS), :]
             a = h * x_ref[pl.ds(chan, SLOTS), :]
             b = h * y_ref[pl.ds(chan, SLOTS), :]
@@ -226,11 +221,25 @@
 
 
 def kernel(
-    count, parts, chans_ref, window_ref, waves_ref, lags_ref, basis_ref, inverse_ref, out_ref,
-    h_ref, x_ref, y_ref, p_ref, q_ref,
+    devices, windows, chans_ref, records_ref, waves_ref, lags_ref, basis_ref, inverse_ref, out_ref,
+    win, send, recv, h_ref, x_ref, y_ref, p_ref, q_ref,
 ):
-    waves_spectra(waves_ref, lags_ref, basis_ref, h_ref, 256)
-    record_spectra(window_ref, basis_ref, x_ref, y_ref, 256)
+    count, parts = chans_ref.shape
+    rows, time_dev = records_ref.shape
+    moves = Gather(win, send, recv, devices, windows, rows, time_dev)
+    chunks = list(range(count // CHUNK))
+
+    def beside():
+        if chunks:
+            waves_spectra(waves_ref, lags_ref, basis_ref, h_ref, parts, chunks.pop(0))
+
+    moves.own(records_ref)
+    moves.greet()
+    moves.run(beside)
+    while chunks:
+        beside()
+    moves.finish()
+    record_spectra(win, basis_ref, x_ref, y_ref, 256)
     correlate(chans_ref, h_ref, x_ref, y_ref, p_ref, q_ref, count, parts)
     back(p_ref, q_ref, inverse_ref, out_ref, count)
 
@@ -254,36 +263,34 @@
     )
     devices, windows = lax.axis_size("tmpl"), lax.axis_size("tm")
     copies = 3 * devices // 2
-    window = pl.pallas_call(
-        functools.partial(gather_kernel, devices, windows),
-        out_shape=jax.ShapeDtypeStruct((devices * records.shape[0], wide), records.dtype),
-        in_specs=[pl.BlockSpec(memory_space=pltpu.VMEM)],
-        out_specs=pl.BlockSpec(memory_space=pltpu.VMEM),
-        scratch_shapes=[
-            pltpu.VMEM((devices * records.shape[0], wide), records.dtype),
-            pltpu.SemaphoreType.DMA((copies,)),
-            pltpu.SemaphoreType.DMA((copies,)),
-        ],
-        compiler_params=pltpu.CompilerParams(
-            collective_id=0, has_side_effects=True, vmem_limit_bytes=24 * 2**20
-        ),
-    )(records)
-    waves = jnp.pad(templates.reshape(rows, L), ((0, 0), (0, SPAN - L)))
+    everyone = devices * records.shape[0]
     vmem = pl.BlockSpec(memory_space=pltpu.VMEM)
     out = pl.pallas_call(
-        functools.partial(kernel, total, parts),
+        functools.partial(kernel, devices, windows),
         out_shape=jax.ShapeDtypeStruct((total, time_dev), jnp.float32),
         in_specs=[pl.BlockSpec(memory_space=pltpu.SMEM)] + [vmem] * 5,
         out_specs=vmem,
         scratch_shapes=[
+            pltpu.VMEM((everyone, wide), records.dtype),
+            pltpu.SemaphoreType.DMA((copies,)),
+            pltpu.SemaphoreType.DMA((copies,)),
             pltpu.VMEM((rows * SLOTS, LANES), jnp.float32),
-            pltpu.VMEM((window.shape[0] * SLOTS, LANES), jnp.float32),
-            pltpu.VMEM((window.shape[0] * SLOTS, LANES), jnp.float32),
+            pltpu.VMEM((everyone * SLOTS, LANES), jnp.float32),
+            pltpu.VMEM((everyone * SLOTS, LANES), jnp.float32),
             pltpu.VMEM((total * SLOTS, LANES), jnp.float32),
             pltpu.VMEM((total * SLOTS, LANES), jnp.float32),
         ],
-        compiler_params=pltpu.CompilerParams(vmem_limit_bytes=52 * 2**20),
-    )(channels.reshape(rows), window, waves, moveouts.reshape(rows, 1), basis, inverse)
+        compiler_params=pltpu.CompilerParams(
+            collective_id=0, has_side_effects=True, vmem_limit_bytes=52 * 2**20
+        ),
+    )(
+        channels.reshape(total, parts),
+        records,
+        templates.reshape(rows, L),
+        moveouts.reshape(total, parts),
+        basis,
+        inverse,
+    )
     return out.reshape(batches, count, time_dev)
 
 

time: 54.9 us -> 44.4 us (0.81)
  Pallas kernels: 47.7 us -> 39.8 us
  local copies, waits for them, and re-layouts: 7.03 us -> 4.33 us
    pallas_call x2 -> x1, Pallas kernels: 47.7 us -> 39.8 us  [per_device(): pl.pallas_call(functools.partial(kernel, devices, windows), out_shape=jax...]
    unnamed x8 -> x9, local copies, waits for them, and re-layouts: 1.43 us -> 4.33 us
    pad x1 -> x0, local copies, waits for them, and re-layouts: 2.82 us -> none  [per_device(): waves = jnp.pad(templates.reshape(rows, L), ((0, 0), (0, SPAN - L)))]
    reshape x2 -> x0, local copies, waits for them, and re-layouts: 2.79 us -> none  [the longest x1 1.96 us: per_device(): moveouts.reshape(rows, 1)]
where the time goes in v3:
time: 44.4 us; the launch traced here: 44.1 us
  Pallas kernels  39.8 us (90%)
  local copies, waits for them, and re-layouts  4.33 us (10%)
    pallas_call x1, Pallas kernels, per_device(): pl.pallas_call(functools.partial(kernel, devices, windows), out_shape=jax...  39.8 us
    unnamed x9, local copies, waits for them, and re-layouts  4.33 us

profile of v3, /device:TPU:0, one launch (start us, length us, event | category | flops | bytes accessed | tf_op | source)
XLA Modules:
  0.0 44.1 jit_solution(4868192030886352531)
XLA Ops:
  0.0 0.0 copy-start
  0.0 1.3 %copy-done = bf16[768,768]{1,0:T(8,128)(2,1)S(1)} copy-done((bf16[768,768]{1,0:T(8,128)(2,1)S(1)}, bf16[768,768]{1,0:T(8,128)(2,1)}, u32[]{:S(2)}) %copy-start) | copy-done | bytes 1179672
  1.3 0.0 copy-start.1
  1.3 0.9 %copy-done.1 = bf16[96,512]{1,0:T(8,128)(2,1)S(1)} copy-done((bf16[96,512]{1,0:T(8,128)(2,1)S(1)}, bf16[96,512]{1,0:T(8,128)(2,1)}, u32[]{:S(2)}) %copy-start.1) | copy-done | bytes 98328
  2.2 0.0 copy-start.2
  2.2 0.8 %copy-done.2 = s32[2,32,48]{2,1,0:T(8,128)S(1)} copy-done((s32[2,32,48]{2,1,0:T(8,128)S(1)}, s32[2,32,48]{2,1,0:T(8,128)}, u32[]{:S(2)}) %copy-start.2) | copy-done | bytes 12312
  2.9 0.0 copy-start.3
  2.9 0.8 %copy-done.3 = s32[2,32,48]{2,1,0:T(8,128)S(1)} copy-done((s32[2,32,48]{2,1,0:T(8,128)S(1)}, s32[2,32,48]{2,1,0:T(8,128)}, u32[]{:S(2)}) %copy-start.3) | copy-done | bytes 12312
  3.7 39.8 %shard_map.64 = f32[64,512]{1,0:T(8,128)S(1)} custom-call(s32[64,48]{1,0:T(8,128)S(1)} %bitcast.5, bf16[96,512]{1,0:T(8,128)(2,1)S(1)} %copy-done.1, bf16[3072,200]{1,0:T(8,128)(2,1)} %bitcast.7, s32[64,48]{1,0:T(8,128)S(1)} %bitcast.6, bf16[768,768]{1,0:T(8,128)(2,1)S(1)} %copy-done, f32[768,512]{1,0:T(8,128)} %constant.5.clone.inverse_ref), custom_call_target="tpu_custom_call" | custom-call | tf_op jit(solution)/shard_map/pallas_call | solution.py:268
  43.5 0.7 %copy.8 = f32[2,32,512]{2,1,0:T(8,128)} copy(f32[2,32,512]{2,1,0:T(8,128)S(1)} %bitcast.4) | data formatting | bytes 262144
Async XLA Ops:
  0.0 1.3 %copy-start = (bf16[768,768]{1,0:T(8,128)(2,1)S(1)}, bf16[768,768]{1,0:T(8,128)(2,1)}, u32[]{:S(2)}) copy-start(bf16[768,768]{1,0:T(8,128)(2,1)} %constant.4.clone.basis_ref) | copy-start | bytes 3538948
  1.3 0.9 %copy-start.1 = (bf16[96,512]{1,0:T(8,128)(2,1)S(1)}, bf16[96,512]{1,0:T(8,128)(2,1)}, u32[]{:S(2)}) copy-start(bf16[96,512]{1,0:T(8,128)(2,1)} %records_ref.1) | copy-start | bytes 294916
  2.2 0.8 %copy-start.2 = (s32[2,32,48]{2,1,0:T(8,128)S(1)}, s32[2,32,48]{2,1,0:T(8,128)}, u32[]{:S(2)}) copy-start(s32[2,32,48]{2,1,0:T(8,128)} %param.8) | copy-start | bytes 36868
  2.9 0.8 %copy-start.3 = (s32[2,32,48]{2,1,0:T(8,128)S(1)}, s32[2,32,48]{2,1,0:T(8,128)}, u32[]{:S(2)}) copy-start(s32[2,32,48]{2,1,0:T(8,128)} %param.9) | copy-start | bytes 36868

commit v4 on v3

--- a/solution.py
+++ b/solution.py
@@ -100,7 +100,7 @@
         at = pl.multiple_of(self.me * self.rows, self.rows)
         self.win[pl.ds(at, self.rows), pl.ds(0, self.time_dev)] = records_ref[...]
 
-    def run(self, beside=lambda: None):
+    def run(self, beside, complete):
         for k in self.turns[1:]:
             self.go(self.main(k, 0))
         for k in self.turns:
@@ -120,18 +120,15 @@
                 beside()
                 self.rim(k, j).wait_recv()
                 self.go(self.across(k, j))
-
-    def finish(self):
+                complete(self.index(k, j, self.core))
+
+    def finish(self, complete):
         for j in range(self.inner):
             for k in self.turns:
                 self.across(k, j).wait_recv()
+                complete(self.index(k, j, 1 - self.core))
         for copy in self.sent:
             copy.wait_send()
-
-        @pl.when(self.tm == self.windows - 1)
-        def _():
-            rim = self.win.shape[0], SPAN
-            self.win[:, pl.ds(self.time_dev, SPAN)] = jnp.zeros(rim, self.win.dtype)
 
 
 def tables(count, freqs, width):
@@ -169,18 +166,17 @@
     spread(h_ref, first, rows, spec, (0, 1, 2, 4, 5, 6))
 
 
-def record_spectra(window_ref, basis_ref, x_ref, y_ref, rows):
-    def step(i, carry):
-        first = pl.multiple_of(i * rows, rows)
-        spec = jnp.dot(
-            window_ref[pl.ds(first, rows), :], basis_ref[...], preferred_element_type=jnp.float32
-        )
-        spec = spec.astype(jnp.bfloat16).astype(jnp.float32)
-        spread(x_ref, first, rows, spec, (0, 1, 2, 4, 5, 6))
-        spread(y_ref, first, rows, spec, (4, 5, 6, 0, 1, 2))
-        return carry
-
-    lax.fori_loop(0, window_ref.shape[0] // rows, step, 0)
+def record_spectra(win, first, rows, time_dev, keep, basis_ref, x_ref, y_ref):
+    at = pl.ds(first, rows)
+    spec = jnp.dot(
+        win[at, :time_dev], basis_ref[:time_dev, :], preferred_element_type=jnp.float32
+    )
+    spec += keep * jnp.dot(
+        win[at, time_dev:], basis_ref[time_dev:, :], preferred_element_type=jnp.float32
+    )
+    spec = spec.astype(jnp.bfloat16).astype(jnp.float32)
+    spread(x_ref, first, rows, spec, (0, 1, 2, 4, 5, 6))
+    spread(y_ref, first, rows, spec, (4, 5, 6, 0, 1, 2))
 
 
 def correlate(chans_ref, h_ref, x_ref, y_ref, p_ref, q_ref, count, parts):
@@ -233,13 +229,18 @@
         if chunks:
             waves_spectra(waves_ref, lags_ref, basis_ref, h_ref, parts, chunks.pop(0))
 
+    keep = jnp.where(moves.tm == windows - 1, 0.0, 1.0).astype(jnp.float32)
+
+    def complete(index):
+        first = pl.multiple_of(index * rows, rows)
+        record_spectra(win, first, rows, time_dev, keep, basis_ref, x_ref, y_ref)
+
     moves.own(records_ref)
     moves.greet()
-    moves.run(beside)
+    moves.run(beside, complete)
     while chunks:
         beside()
-    moves.finish()
-    record_spectra(win, basis_ref, x_ref, y_ref, 256)
+    moves.finish(complete)
     correlate(chans_ref, h_ref, x_ref, y_ref, p_ref, q_ref, count, parts)
     back(p_ref, q_ref, inverse_ref, out_ref, count)
 

time: 44.4 us -> 44 us (level)
  no operation moved by 1% of the time
where the time goes in v4:
time: 44 us; the launch traced here: 43.7 us
  Pallas kernels  39.4 us (90%)
  local copies, waits for them, and re-layouts  4.33 us (10%)
    pallas_call x1, Pallas kernels, per_device(): pl.pallas_call(functools.partial(kernel, devices, windows), out_shape=jax...  39.4 us
    unnamed x9, local copies, waits for them, and re-layouts  4.33 us

profile of v4, /device:TPU:0, one launch (start us, length us, event | category | flops | bytes accessed | tf_op | source)
XLA Modules:
  0.0 43.7 jit_solution(9933866421477651254)
XLA Ops:
  0.0 0.0 copy-start
  0.0 1.3 %copy-done = bf16[768,768]{1,0:T(8,128)(2,1)S(1)} copy-done((bf16[768,768]{1,0:T(8,128)(2,1)S(1)}, bf16[768,768]{1,0:T(8,128)(2,1)}, u32[]{:S(2)}) %copy-start) | copy-done | bytes 1179672
  1.3 0.0 copy-start.1
  1.3 0.9 %copy-done.1 = bf16[96,512]{1,0:T(8,128)(2,1)S(1)} copy-done((bf16[96,512]{1,0:T(8,128)(2,1)S(1)}, bf16[96,512]{1,0:T(8,128)(2,1)}, u32[]{:S(2)}) %copy-start.1) | copy-done | bytes 98328
  2.2 0.0 copy-start.2
  2.2 0.8 %copy-done.2 = s32[2,32,48]{2,1,0:T(8,128)S(1)} copy-done((s32[2,32,48]{2,1,0:T(8,128)S(1)}, s32[2,32,48]{2,1,0:T(8,128)}, u32[]{:S(2)}) %copy-start.2) | copy-done | bytes 12312
  2.9 0.0 copy-start.3
  2.9 0.8 %copy-done.3 = s32[2,32,48]{2,1,0:T(8,128)S(1)} copy-done((s32[2,32,48]{2,1,0:T(8,128)S(1)}, s32[2,32,48]{2,1,0:T(8,128)}, u32[]{:S(2)}) %copy-start.3) | copy-done | bytes 12312
  3.7 39.4 %shard_map.64 = f32[64,512]{1,0:T(8,128)S(1)} custom-call(s32[64,48]{1,0:T(8,128)S(1)} %bitcast.5, bf16[96,512]{1,0:T(8,128)(2,1)S(1)} %copy-done.1, bf16[3072,200]{1,0:T(8,128)(2,1)} %bitcast.7, s32[64,48]{1,0:T(8,128)S(1)} %bitcast.6, bf16[768,768]{1,0:T(8,128)(2,1)S(1)} %copy-done, f32[768,512]{1,0:T(8,128)} %constant.5.clone.inverse_ref), custom_call_target="tpu_custom_call" | custom-call | tf_op jit(solution)/shard_map/pallas_call | solution.py:269
  43.1 0.7 %copy.8 = f32[2,32,512]{2,1,0:T(8,128)} copy(f32[2,32,512]{2,1,0:T(8,128)S(1)} %bitcast.4) | data formatting | bytes 262144
Async XLA Ops:
  0.0 1.3 %copy-start = (bf16[768,768]{1,0:T(8,128)(2,1)S(1)}, bf16[768,768]{1,0:T(8,128)(2,1)}, u32[]{:S(2)}) copy-start(bf16[768,768]{1,0:T(8,128)(2,1)} %constant.4.clone.basis_ref) | copy-start | bytes 3538948
  1.3 0.9 %copy-start.1 = (bf16[96,512]{1,0:T(8,128)(2,1)S(1)}, bf16[96,512]{1,0:T(8,128)(2,1)}, u32[]{:S(2)}) copy-start(bf16[96,512]{1,0:T(8,128)(2,1)} %records_ref.1) | copy-start | bytes 294916
  2.2 0.8 %copy-start.2 = (s32[2,32,48]{2,1,0:T(8,128)S(1)}, s32[2,32,48]{2,1,0:T(8,128)}, u32[]{:S(2)}) copy-start(s32[2,32,48]{2,1,0:T(8,128)} %param.8) | copy-start | bytes 36868
  2.9 0.8 %copy-start.3 = (s32[2,32,48]{2,1,0:T(8,128)S(1)}, s32[2,32,48]{2,1,0:T(8,128)}, u32[]{:S(2)}) copy-start(s32[2,32,48]{2,1,0:T(8,128)} %param.9) | copy-start | bytes 36868

commit v5 on v4

--- a/solution.py
+++ b/solution.py
@@ -217,15 +217,23 @@
 
 
 def kernel(
-    devices, windows, chans_ref, records_ref, waves_ref, lags_ref, basis_ref, inverse_ref, out_ref,
-    win, send, recv, h_ref, x_ref, y_ref, p_ref, q_ref,
+    devices, windows, chans_ref, records_ref, lags_ref, waves_far, basis_far, inverse_far, out_ref,
+    waves_ref, basis_ref, inverse_ref, load, win, send, recv, h_ref, x_ref, y_ref, p_ref, q_ref,
 ):
     count, parts = chans_ref.shape
     rows, time_dev = records_ref.shape
     moves = Gather(win, send, recv, devices, windows, rows, time_dev)
     chunks = list(range(count // CHUNK))
 
+    pairs = ((waves_far, waves_ref), (basis_far, basis_ref), (inverse_far, inverse_ref))
+    loads = [pltpu.make_async_copy(a, b, load.at[i]) for i, (a, b) in enumerate(pairs)]
+    for copy in loads:
+        copy.start()
+    pending = loads[:2]
+
     def beside():
+        while pending:
+            pending.pop(0).wait()
         if chunks:
             waves_spectra(waves_ref, lags_ref, basis_ref, h_ref, parts, chunks.pop(0))
 
@@ -242,6 +250,7 @@
         beside()
     moves.finish(complete)
     correlate(chans_ref, h_ref, x_ref, y_ref, p_ref, q_ref, count, parts)
+    loads[2].wait()
     back(p_ref, q_ref, inverse_ref, out_ref, count)
 
 
@@ -269,9 +278,13 @@
     out = pl.pallas_call(
         functools.partial(kernel, devices, windows),
         out_shape=jax.ShapeDtypeStruct((total, time_dev), jnp.float32),
-        in_specs=[pl.BlockSpec(memory_space=pltpu.SMEM)] + [vmem] * 5,
+        in_specs=[pl.BlockSpec(memory_space=pltpu.SMEM)] + [vmem] * 2 + [pl.BlockSpec(memory_space=pl.ANY)] * 3,
         out_specs=vmem,
         scratch_shapes=[
+            pltpu.VMEM((rows, L), templates.dtype),
+            pltpu.VMEM(basis.shape, basis.dtype),
+            pltpu.VMEM(inverse.shape, inverse.dtype),
+            pltpu.SemaphoreType.DMA((3,)),
             pltpu.VMEM((everyone, wide), records.dtype),
             pltpu.SemaphoreType.DMA((copies,)),
             pltpu.SemaphoreType.DMA((copies,)),
@@ -282,13 +295,13 @@
             pltpu.VMEM((total * SLOTS, LANES), jnp.float32),
         ],
         compiler_params=pltpu.CompilerParams(
-            collective_id=0, has_side_effects=True, vmem_limit_bytes=52 * 2**20
+            collective_id=0, has_side_effects=True, vmem_limit_bytes=56 * 2**20
         ),
     )(
         channels.reshape(total, parts),
         records,
+        moveouts.reshape(total, parts),
         templates.reshape(rows, L),
-        moveouts.reshape(total, parts),
         basis,
         inverse,
     )

time: 44 us -> 41.1 us (0.934)
  local copies, waits for them, and re-layouts: 4.33 us -> 1.57 us
    unnamed x9 -> x1, local copies, waits for them, and re-layouts: 4.33 us -> 1.57 us
where the time goes in v5:
time: 41.1 us; the launch traced here: 40.9 us
  Pallas kernels  39.3 us (96%)
  local copies, waits for them, and re-layouts  1.57 us (4%)
    pallas_call x1, Pallas kernels, per_device(): pl.pallas_call(functools.partial(kernel, devices, windows), out_shape=jax...  39.3 us
    unnamed x1, local copies, waits for them, and re-layouts  1.57 us

profile of v5, /device:TPU:0, one launch (start us, length us, event | category | flops | bytes accessed | tf_op | source)
XLA Modules:
  0.0 40.9 jit_solution(11525457470969906239)
XLA Ops:
  0.0 39.3 %shard_map.64 = f32[64,512]{1,0:T(8,128)} custom-call(s32[64,48]{1,0:T(8,128)} %bitcast.6, bf16[96,512]{1,0:T(8,128)(2,1)} %records_ref.1, s32[64,48]{1,0:T(8,128)} %bitcast.7, bf16[3072,200]{1,0:T(8,128)(2,1)} %bitcast.4, bf16[768,768]{1,0:T(8,128)(2,1)} %constant.4.clone.basis_far, f32[768,512]{1,0:T(8,128)} %constant.5.clone.inverse_far), custom_call_target="tpu_custom_call" | custom-call | tf_op jit(solution)/shard_map/pallas_call | solution.py:278
  39.3 1.6 %copy.8 = f32[2,32,512]{2,1,0:T(8,128)} copy(f32[2,32,512]{2,1,0:T(8,128)} %bitcast.5) | data formatting | bytes 262144
